TPU v7x, 32 devices: a whole 2x2x4 slice. The times are simulated.
32 devices in a mesh: row: 8 (over y, x, core), col: 4 (over z).
Axes of the slice: x: 2, y: 2, z: 4, core: 2. Of those that a mesh axis runs over, the one named last changes fastest.
Arguments:
- adjoint: float32 [3, 512, 256, 256], P(None, 'row', 'col'), may hold values from -6 to 6
- gradients: bfloat16 [9, 384, 768, 384], P(None, 'row', 'col'), may hold values from -6 to 6
Outputs:
- forcing: float32 [3, 512, 256, 256], P(None, 'row', 'col')
All inputs are finite; a program needn't handle non-finite values.
Results may differ from a plain program's by a relative error of at most 0.0003.
Values sent between devices are 32-bit elements; how exact they have to be, the bound alone decides.
A program may use at most 384 MiB of HBM per device.

v0:
```python
import math

import jax
import jax.numpy as jnp
from jax import lax
from jax.sharding import PartitionSpec as P

KR = 256
KT = 512
KZ = 256
NR = 384
NT = 768
NZ = 384


def wave_table(points, modes):
    positions = jnp.arange(points, dtype=jnp.int32)[:, None]
    indices = jnp.arange(modes, dtype=jnp.int32)[None, :]
    wavenumber = (indices + 1) // 2
    angles = (positions * wavenumber % points).astype(jnp.float32) * (2.0 * math.pi / points)
    return jnp.where(
        indices % 2 == 1,
        jnp.cos(angles),
        jnp.where(indices == 0, jnp.ones_like(angles), jnp.sin(angles)),
    )


def fourier_inverse(points, modes):
    return wave_table(points, modes) * (1.0 / math.sqrt(modes))


def fourier_forward(points, modes):
    indices = jnp.arange(modes, dtype=jnp.int32)
    weights = jnp.where(indices == 0, 1.0, 2.0).astype(jnp.float32) * (math.sqrt(modes) / points)
    return wave_table(points, modes).T * weights[:, None]


def cosine_table(points, modes):
    positions = jnp.arange(points, dtype=jnp.int32)[:, None]
    indices = jnp.arange(modes, dtype=jnp.int32)[None, :]
    angles = (indices * (2 * positions + 1) % (4 * points)).astype(jnp.float32) * (
        math.pi / (2 * points)
    )
    return jnp.cos(angles)


def chebyshev_inverse(points, modes):
    return cosine_table(points, modes) * (1.0 / math.sqrt(modes))


def chebyshev_forward(points, modes):
    indices = jnp.arange(modes, dtype=jnp.int32)
    weights = jnp.where(indices == 0, 1.0, 2.0).astype(jnp.float32) * (math.sqrt(modes) / points)
    return cosine_table(points, modes).T * weights[:, None]


def per_device(adjoint, gradients):
    highest = lax.Precision.HIGHEST
    kt_local = adjoint.shape[1]
    kz_local = adjoint.shape[2]
    rows_here = gradients.shape[1]
    columns_here = gradients.shape[2]
    col_count = lax.axis_size("col")
    theta_inverse = fourier_inverse(NT, KT)
    axial_inverse = fourier_inverse(NZ, KZ)
    theta_forward = fourier_forward(NT, KT)
    axial_forward = fourier_forward(NZ, KZ)
    radial_forward = chebyshev_forward(NR, KR)
    radial = jnp.einsum("ftzk,jk->ftzj", adjoint, chebyshev_inverse(NR, KR), precision=highest)
    outbound = jnp.transpose(radial, (0, 1, 3, 2)).reshape(3, kt_local, NR * kz_local)
    turned = jnp.einsum(
        "fka,sk->fsa",
        lax.all_to_all(outbound, "row", split_axis=2, concat_axis=1, tiled=True),
        theta_inverse,
        precision=highest,
    )
    arrived = lax.all_to_all(turned, "col", split_axis=1, concat_axis=2, tiled=True)
    members = arrived.shape[0]
    layered = arrived.reshape(members, columns_here, col_count, rows_here, kz_local)
    ordered = jnp.transpose(layered, (0, 1, 3, 2, 4)).reshape(members, columns_here, rows_here, KZ)
    velocity = jnp.einsum("fsrk,qk->frsq", ordered, axial_inverse, precision=highest)
    outputs = []
    for target in range(3):
        total = gradients[target].astype(jnp.float32) * velocity[0]
        for source in range(1, 3):
            total = total + gradients[3 * source + target].astype(jnp.float32) * velocity[source]
        outputs.append(total)
    product = jnp.stack(outputs)
    axial = jnp.einsum("frsq,kq->fsrk", product, axial_forward, precision=highest)
    layered = axial.reshape(3, columns_here, rows_here, col_count, kz_local)
    returning = jnp.transpose(layered, (0, 1, 3, 2, 4)).reshape(
        3, columns_here, col_count * rows_here * kz_local
    )
    middle = jnp.einsum(
        "fsa,ks->fka",
        lax.all_to_all(returning, "col", split_axis=2, concat_axis=1, tiled=True),
        theta_forward,
        precision=highest,
    )
    arrived = lax.all_to_all(middle, "row", split_axis=1, concat_axis=2, tiled=True)
    members = arrived.shape[0]
    shaped = arrived.reshape(members, kt_local, NR, kz_local)
    ordered = jnp.transpose(shaped, (0, 1, 3, 2))
    return jnp.einsum("ftzj,kj->ftzk", ordered, radial_forward, precision=highest)


def solution(mesh):
    placed = (P(None, "row", "col", None), P(None, "row", "col", None))
    return jax.shard_map(
        per_device,
        mesh=mesh,
        in_specs=placed,
        out_specs=P(None, "row", "col", None),
        check_vma=False,
    )
```

profile of v0, /device:TPU:9, one launch (start us, length us, event | category | flops | bytes accessed | tf_op | source)
XLA Modules:
  0.0 3415.3 jit_solution(4969472096886941073)
XLA Ops:
  0.0 0.6 copy-done
  0.6 30.7 convolution_bitcast_fusion.2
  31.3 41.6 %copy.52 = f32[3,64,384,64]{1,0,3,2:T(4,128)} copy(f32[3,64,384,64]{2,3,1,0:T(8,128)} %convolution_bitcast_fusion.2) | data formatting | bytes 37748736 | tf_op jit(solution)/shard_map/reshape | solution.py:70
  72.9 69.5 %reshape.171 = f32[8,1,589824]{2,1,0:T(1,128)} reshape(f32[24576,3,64]{2,1,0:T(4,128)} %bitcast.91) | data formatting | bytes 37748736
  142.4 6.5 all-to-all-start
  148.9 0.0 copy-start.4
  148.9 0.0 copy-start.6
  148.9 0.0 copy-start.2
  149.0 0.5 copy-done.4
  149.4 0.0 copy-done.6
  149.5 0.1 copy-done.2
  149.5 6.5 fusion.174
  156.0 195.8 %all-to-all-done = f32[8,1,589824]{2,1,0:T(1,128)} async-done(((f32[8,1,589824]{2,1,0:T(1,128)}), f32[8,1,589824]{2,1,0:T(1,128)}, u32[]{:S(2)}, u32[]{:S(2)}) %all-to-all-start) | async-done | bytes 18874400 | tf_op jit(solution)/shard_map/all_to_all | solution.py:73
  351.8 0.6 broadcast.363
  352.4 54.1 %reduce = f32[8,589824]{1,0:T(8,128)} reduce(f32[8,1,589824]{2,1,0:T(1,128)} %all-to-all-done, f32[]{:T(128)} %broadcast.363), dimensions={1}, to_apply=%all_to_all.48.reduce_sub_computation | reduce | bytes 37748740 | tf_op jit(solution)/shard_map/all_to_all | solution.py:73
  406.5 77.4 %reshape.172 = f32[24576,3,64]{2,1,0:T(4,128)} reshape(f32[8,589824]{1,0:T(8,128)} %reduce) | data formatting | bytes 37748736
  483.9 39.1 %copy.54 = f32[3,64,8,3072]{3,1,2,0:T(8,128)} copy(f32[3,64,8,3072]{1,0,3,2:T(4,128)} %bitcast.92) | data formatting | bytes 37748736 | tf_op jit(solution)/shard_map/all_to_all | solution.py:73
  523.0 50.5 %convolution_bitcast_fusion.1 = f32[3,768,3072]{2,1,0:T(8,128)} fusion(f32[3,512,3072]{2,1,0:T(8,128)} %bitcast.101, f32[768,512,1]{1,0,2:T(8,128)S(1)} %fusion.174), kind=kOutput, calls=%fused_computation.14 | convolution fusion | flops 43486543872 | bytes 48758784 | tf_op jit(solution)/shard_map/fka,sk->fsa/dot_general | solution.py:71
  573.5 37.8 %copy.34 = f32[3,768,3072]{2,0,1:T(4,128)} copy(f32[3,768,3072]{2,1,0:T(8,128)} %convolution_bitcast_fusion.1) | data formatting | bytes 56623104 | tf_op jit(solution)/shard_map/fka,sk->fsa/transpose | solution.py:71
  611.3 10.5 all-to-all-start.1
  621.9 0.0 copy-start.8
  621.9 1.6 fusion.172
  623.5 804.2 %all-to-all-done.1 = f32[3,768,3072]{2,0,1:T(4,128)} async-done(((f32[3,768,3072]{2,0,1:T(4,128)}), f32[3,768,3072]{2,0,1:T(4,128)}, u32[]{:S(2)}, u32[]{:S(2)}) %all-to-all-start.1) | async-done | bytes 28311584 | tf_op jit(solution)/shard_map/all_to_all | solution.py:77
  1427.7 29.2 copy.35
  1456.9 32.8 copy.36
  1489.7 27.6 copy.37
  1517.3 66.6 %convolution_bitcast_fusion = f32[3,48,192,384]{3,2,1,0:T(8,128)} fusion(f32[3,192,48,256]{1,3,2,0:T(8,128)} %bitcast.93, f32[384,256,1,1]{1,0,3,2:T(8,128)S(1)} %fusion.172), kind=kOutput, calls=%fused_computation.6 | convolution fusion | flops 32614907904 | bytes 71172096 | tf_op jit(solution)/shard_map/fsrk,qk->frsq/dot_general | solution.py:81
  1583.9 48.6 %multiply_add_fusion.2 = (f32[1,48,192,384]{3,2,1,0:T(8,128)}, f32[1,48,192,384]{3,2,1,0:T(8,128)}, f32[1,48,192,384]{3,2,1,0:T(8,128)}) fusion(f32[3,48,192,384]{3,2,1,0:T(8,128)} %convolution_bitcast_fusion, bf16[9,48,192,384]{3,2,1,0:T(8,128)(2,1)} %param.3), kind=kLoop, calls=%fused_computation.12 | loop fusion | flops 84934656 | bytes 148635648 | tf_op jit(solution)/shard_map/add | solution.py:86
  1632.5 0.0 copy-done.8
  1632.5 62.6 %fusion.8 = f32[3,192,48,256]{3,1,2,0:T(8,128)} fusion(f32[1,48,192,384]{3,2,1,0:T(8,128)} %get-tuple-element.7, f32[1,48,192,384]{3,2,1,0:T(8,128)} %get-tuple-element.6, f32[1,48,192,384]{3,2,1,0:T(8,128)} %get-tuple-element.5, f32[256]{0:T(256)S(1)} %select_multiply_fusion.1, s32[256]{0:T(256)S(1)} %and_select_fusion, ...), kind=kOutput, calls=%fused_computation.13 | convolution fusion | flops 32637321216 | bytes 70781440 | tf_op jit(solution)/shard_map/frsq,kq->fsrk/dot_general | solution.py:89
  1695.2 32.6 copy.39
  1727.8 27.4 copy.40
  1755.2 49.0 %copy.41 = f32[3,192,12288]{1,0,2:T(4,128)} copy(f32[3,192,12288]{1,2,0:T(8,128)} %bitcast.96) | data formatting | bytes 56623104 | tf_op jit(solution)/shard_map/reshape | solution.py:91
  1804.2 0.0 copy-start.7
  1804.2 17.9 all-to-all-start.2
  1822.1 0.0 copy-done.3
  1822.1 0.0 copy-done.5
  1822.1 8.2 fusion.176
  1830.2 1069.2 %all-to-all-done.2 = f32[3,192,12288]{1,0,2:T(4,128)} async-done(((f32[3,192,12288]{1,0,2:T(4,128)}), f32[3,192,12288]{1,0,2:T(4,128)}, u32[]{:S(2)}, u32[]{:S(2)}) %all-to-all-start.2) | async-done | bytes 28311584 | tf_op jit(solution)/shard_map/all_to_all | solution.py:96
  2899.5 44.1 %copy.43 = f32[3,4,192,3072]{3,2,1,0:T(8,128)} copy(f32[3,4,192,3072]{2,0,3,1:T(4,128)} %bitcast.27) | data formatting | bytes 56623104 | tf_op jit(solution)/shard_map/all_to_all | solution.py:96
  2943.6 50.0 %convolution_bitcast_fusion.3 = f32[3,512,3072]{2,1,0:T(8,128)S(1)} fusion(f32[3,768,3072]{2,1,0:T(8,128)} %bitcast.97, f32[512,768,1]{1,0,2:T(8,128)} %fusion.176), kind=kOutput, calls=%fused_computation.16 | convolution fusion | flops 43486543872 | bytes 48758784 | tf_op jit(solution)/shard_map/fsa,ks->fka/dot_general | solution.py:94
  2993.6 34.5 %copy.44 = f32[3,512,3072]{2,0,1:T(4,128)S(1)} copy(f32[3,512,3072]{2,1,0:T(8,128)S(1)} %convolution_bitcast_fusion.3) | data formatting | bytes 37748736 | tf_op jit(solution)/shard_map/fsa,ks->fka/transpose | solution.py:94
  3028.1 280.3 %all_to_all.66 = f32[3,512,3072]{2,0,1:T(4,128)} all-to-all(f32[3,512,3072]{2,0,1:T(4,128)S(1)} %copy.44), channel_id=1, replica_groups=mesh['row'=8,'col'=4] {'row'}, dimensions={1} | all-to-all | bytes 37748736 | tf_op jit(solution)/shard_map/all_to_all | solution.py:100
  3308.4 20.9 copy.59
  3329.3 27.4 reshape.164
  3356.7 27.7 copy.46
  3384.4 0.0 copy-done.1
  3384.4 30.7 fusion.6
  (14 shorter events, 0.0 us)
Async XLA Ops:
  0.0 0.6 copy-start
  142.4 209.4 %all-to-all-start = ((f32[8,1,589824]{2,1,0:T(1,128)}), f32[8,1,589824]{2,1,0:T(1,128)}, u32[]{:S(2)}, u32[]{:S(2)}) async-start(f32[8,1,589824]{2,1,0:T(1,128)} %reshape.171), calls=%async_computation | async-start | bytes 37748736 | tf_op jit(solution)/shard_map/all_to_all | solution.py:73
  148.9 0.5 copy-start.4
  148.9 0.5 copy-start.6
  148.9 0.6 copy-start.2
  611.3 816.4 %all-to-all-start.1 = ((f32[3,768,3072]{2,0,1:T(4,128)}), f32[3,768,3072]{2,0,1:T(4,128)}, u32[]{:S(2)}, u32[]{:S(2)}) async-start(f32[3,768,3072]{2,0,1:T(4,128)} %copy.34), calls=%async_computation.1 | async-start | bytes 75497472 | tf_op jit(solution)/shard_map/all_to_all | solution.py:77
  621.9 1010.6 %copy-start.8 = (f32[256]{0:T(256)}, f32[256]{0:T(256)S(1)}, u32[]{:S(2)}) copy-start(f32[256]{0:T(256)S(1)} %select_multiply_fusion.1) | copy-start | bytes 3076
  1804.2 17.9 copy-start.3
  1804.2 17.9 copy-start.5
  1804.2 17.9 copy-start.7
  1804.2 1095.2 %all-to-all-start.2 = ((f32[3,192,12288]{1,0,2:T(4,128)}), f32[3,192,12288]{1,0,2:T(4,128)}, u32[]{:S(2)}, u32[]{:S(2)}) async-start(f32[3,192,12288]{1,0,2:T(4,128)} %copy.41), calls=%async_computation.2 | async-start | bytes 100663296 | tf_op jit(solution)/shard_map/all_to_all | solution.py:96
  3356.7 27.7 copy-start.1
  3356.7 27.7 copy-start.9
where the time goes:
time: 3430 us; the launch traced here: 3420 us
  waiting for transfers between devices  2070 us (60%)
  local copies, waits for them, and re-layouts  620 us (18%)
  matrix products  291 us (8%)
  blocking collectives  280 us (8%)
  other arithmetic  119 us (3%)
  starting transfers between devices  34.8 us (1%)
    all_to_all x1, waiting for transfers between devices, per_device(): lax.all_to_all(returning, 'col', split_axis=2, concat_axis=1, tiled=True)  1070 us
    all_to_all x1, waiting for transfers between devices, per_device(): lax.all_to_all(turned, 'col', split_axis=1, concat_axis=2, tiled=True)  804 us
    all_to_all x1, blocking collectives, per_device(): lax.all_to_all(middle, 'row', split_axis=1, concat_axis=2, tiled=True)  280 us
    all_to_all x1, waiting for transfers between devices, per_device(): lax.all_to_all(outbound, 'row', split_axis=2, concat_axis=1, tiled=True)  196 us
    unnamed x22, local copies, waits for them, and re-layouts  148 us
  transfers between devices with their start and end apart: 3, of which 3 were waited for; matrix products, arithmetic and copies ran while one was open for 0% of the time, Pallas kernels for 0%

commit v1 on v0

v1 whole, which is shorter than its diff:
```python
import functools
import math

import jax
import jax.numpy as jnp
from jax import lax
from jax.experimental import pallas as pl
from jax.experimental.pallas import tpu as pltpu
from jax.sharding import PartitionSpec as P

KR = 256
KT = 512
KZ = 256
NR = 384
NT = 768
NZ = 384


def wave_table(points, modes):
    positions = jnp.arange(points, dtype=jnp.int32)[:, None]
    indices = jnp.arange(modes, dtype=jnp.int32)[None, :]
    wavenumber = (indices + 1) // 2
    angles = (positions * wavenumber % points).astype(jnp.float32) * (2.0 * math.pi / points)
    return jnp.where(
        indices % 2 == 1,
        jnp.cos(angles),
        jnp.where(indices == 0, jnp.ones_like(angles), jnp.sin(angles)),
    )


def fourier_inverse(points, modes):
    return wave_table(points, modes) * (1.0 / math.sqrt(modes))


def fourier_forward(points, modes):
    indices = jnp.arange(modes, dtype=jnp.int32)
    weights = jnp.where(indices == 0, 1.0, 2.0).astype(jnp.float32) * (math.sqrt(modes) / points)
    return wave_table(points, modes).T * weights[:, None]


def cosine_table(points, modes):
    positions = jnp.arange(points, dtype=jnp.int32)[:, None]
    indices = jnp.arange(modes, dtype=jnp.int32)[None, :]
    angles = (indices * (2 * positions + 1) % (4 * points)).astype(jnp.float32) * (
        math.pi / (2 * points)
    )
    return jnp.cos(angles)


def chebyshev_inverse(points, modes):
    return cosine_table(points, modes) * (1.0 / math.sqrt(modes))


def chebyshev_forward(points, modes):
    indices = jnp.arange(modes, dtype=jnp.int32)
    weights = jnp.where(indices == 0, 1.0, 2.0).astype(jnp.float32) * (math.sqrt(modes) / points)
    return cosine_table(points, modes).T * weights[:, None]


MESH = pl.DeviceIdType.MESH
HIGH = lax.Precision.HIGH


def exchange_kernel(plans, *refs):
    parts = len(plans)
    sources, targets = refs[:parts], refs[parts : 2 * parts]
    send_sem, recv_sem, local_sem = refs[2 * parts :]
    barrier = pltpu.get_barrier_semaphore()
    total = 0
    for axis, count, _ in plans:
        me = lax.axis_index(axis)
        for step in range(1, count):
            peer = lax.rem(me + step, count)
            pl.semaphore_signal(barrier, inc=1, device_id={axis: peer}, device_id_type=MESH)
            total += 1
    pl.semaphore_wait(barrier, total)
    copies = []
    slot = 0
    for number, (axis, count, width) in enumerate(plans):
        me = lax.axis_index(axis)
        source, target = sources[number], targets[number]

        def piece(peer):
            if width is None:
                return source.at[peer]
            return source.at[:, pl.ds(pl.multiple_of(peer * width, 128), width)]

        for step in range(1, count):
            peer = lax.rem(me + step, count)
            copy = pltpu.make_async_remote_copy(
                src_ref=piece(peer),
                dst_ref=target.at[me],
                send_sem=send_sem.at[slot],
                recv_sem=recv_sem.at[slot],
                device_id={axis: peer},
                device_id_type=MESH,
            )
            copy.start()
            copies.append(copy)
            slot += 1
        own = pltpu.make_async_copy(piece(me), target.at[me], local_sem.at[number])
        own.start()
        copies.append(own)
    for copy in copies:
        copy.wait()


def exchange(ident, *parts):
    plans, shapes, total = [], [], 0
    for array, axis, width in parts:
        count = lax.axis_size(axis)
        total += count - 1
        plans.append((axis, count, width))
        shape = array.shape if width is None else (count, array.shape[0], width)
        shapes.append(jax.ShapeDtypeStruct(shape, array.dtype))
    return pl.pallas_call(
        functools.partial(exchange_kernel, tuple(plans)),
        out_shape=shapes,
        in_specs=[pl.BlockSpec(memory_space=pl.ANY)] * len(parts),
        out_specs=[pl.BlockSpec(memory_space=pl.ANY)] * len(parts),
        scratch_shapes=[
            pltpu.SemaphoreType.DMA((total,)),
            pltpu.SemaphoreType.DMA((total,)),
            pltpu.SemaphoreType.DMA((len(parts),)),
        ],
        compiler_params=pltpu.CompilerParams(collective_id=ident, has_side_effects=True),
    )(*[array for array, _, _ in parts])


def per_device(adjoint, gradients):
    kt_local = adjoint.shape[1]
    kz_local = adjoint.shape[2]
    rows_here = gradients.shape[1]
    columns_here = gradients.shape[2]
    row_count = lax.axis_size("row")
    col_count = lax.axis_size("col")
    width = rows_here * kz_local
    theta_inverse = fourier_inverse(NT, KT)
    axial_inverse = fourier_inverse(NZ, KZ)
    theta_forward = fourier_forward(NT, KT)
    axial_forward = fourier_forward(NZ, KZ)
    radial_forward = chebyshev_forward(NR, KR)
    radial_inverse = chebyshev_inverse(NR, KR)

    def first(f):
        radial = jnp.einsum("tzk,jk->tjz", adjoint[f], radial_inverse, precision=HIGH)
        return radial.reshape(kt_local, NR * kz_local), "row", width

    def second(gathered):
        turned = jnp.einsum("ka,sk->sa", gathered.reshape(KT, width), theta_inverse, precision=HIGH)
        return turned.reshape(col_count, columns_here, width), "col", None

    def third(arrived):
        layered = arrived.reshape(col_count, columns_here, rows_here, kz_local)
        ordered = jnp.transpose(layered, (1, 2, 0, 3)).reshape(columns_here, rows_here, KZ)
        return jnp.einsum("srk,qk->rsq", ordered, axial_inverse, precision=HIGH)

    (a0,) = exchange(1, first(0))
    a1, b0 = exchange(2, first(1), second(a0))
    a2, b1 = exchange(3, first(2), second(a1))
    (b2,) = exchange(4, second(a2))
    velocity = [third(b0), third(b1), third(b2)]

    def fourth(target):
        total = gradients[target].astype(jnp.float32) * velocity[0]
        for source in range(1, 3):
            total = total + gradients[3 * source + target].astype(jnp.float32) * velocity[source]
        axial = jnp.einsum("rsq,kq->srk", total, axial_forward, precision=HIGH)
        layered = axial.reshape(columns_here, rows_here, col_count, kz_local)
        returning = jnp.transpose(layered, (2, 0, 1, 3)).reshape(col_count, columns_here, width)
        return returning, "col", None

    def fifth(arrived):
        middle = jnp.einsum("sa,ks->ka", arrived.reshape(NT, width), theta_forward, precision=HIGH)
        return middle.reshape(row_count, kt_local, width), "row", None

    def sixth(arrived):
        shaped = arrived.reshape(row_count, kt_local, rows_here, kz_local)
        ordered = jnp.transpose(shaped, (1, 3, 0, 2)).reshape(kt_local, kz_local, NR)
        return jnp.einsum("tzj,kj->tzk", ordered, radial_forward, precision=HIGH)

    (c0,) = exchange(5, fourth(0))
    c1, d0 = exchange(6, fourth(1), fifth(c0))
    c2, d1 = exchange(7, fourth(2), fifth(c1))
    (d2,) = exchange(8, fifth(c2))
    return jnp.stack([sixth(d0), sixth(d1), sixth(d2)])


def solution(mesh):
    placed = (P(None, "row", "col", None), P(None, "row", "col", None))
    return jax.shard_map(
        per_device,
        mesh=mesh,
        in_specs=placed,
        out_specs=P(None, "row", "col", None),
        check_vma=False,
    )
```

time: 3430 us -> 2110 us (0.62)
  waiting for transfers between devices: 2070 us -> 0 us
  Pallas kernels: 0 us -> 1380 us
  blocking collectives: 280 us -> 0 us
  local copies, waits for them, and re-layouts: 620 us -> 353 us
  other arithmetic: 119 us -> 12.1 us
  matrix products: 291 us -> 354 us
  starting transfers between devices: 34.8 us -> 0 us
    all_to_all x3 -> x0, waiting for transfers between devices: 2070 us -> none  [the longest x1 1070 us: per_device(): lax.all_to_all(returning, 'col', split_axis=2, concat_axis=1, tiled=True)]
    pallas_call x0 -> x8, Pallas kernels: none -> 1380 us  [exchange(): pl.pallas_call(functools.partial(exchange_kernel, tuple(plans)), out_shap...]
    all_to_all x1 -> x0, blocking collectives: 280 us -> none  [per_device(): lax.all_to_all(middle, 'row', split_axis=1, concat_axis=2, tiled=True)]
    all_to_all x6 -> x0, local copies, waits for them, and re-layouts: 167 us -> none  [the longest x2 62 us: per_device(): lax.all_to_all(turned, 'col', split_axis=1, concat_axis=2, tiled=True)]
    unnamed x22 -> x14, local copies, waits for them, and re-layouts: 148 us -> 0.03 us
    dot_general x6 -> x18, matrix products: 291 us -> 354 us  [the longest x3 86.4 us: third(): return jnp.einsum('srk,qk->rsq', ordered, axial_inverse, precision=HIGH)]
    all_to_all x1 -> x0, other arithmetic: 54.1 us -> none  [per_device(): lax.all_to_all(outbound, 'row', split_axis=2, concat_axis=1, tiled=True)]
    add x1 -> x0, other arithmetic: 48.6 us -> none  [per_device(): total + gradients[3 * source + target].astype(jnp.float32) * velocity[sou...]
  transfers between devices with their start and end apart: 3 -> 0, of which waited for: 3 -> 0; matrix products, arithmetic and copies ran while one was open for 0% -> 0% of each run, Pallas kernels for 0% -> 0%
where the time goes in v1:
time: 2110 us; the launch traced here: 2100 us
  Pallas kernels  1380 us (65%)
  matrix products  354 us (17%)
  local copies, waits for them, and re-layouts  353 us (17%)
    pallas_call x8, Pallas kernels, exchange(): pl.pallas_call(functools.partial(exchange_kernel, tuple(plans)), out_shap...  1380 us
    dot_general x3, matrix products, third(): return jnp.einsum('srk,qk->rsq', ordered, axial_inverse, precision=HIGH)  86.4 us
    dot_general x3, matrix products, fourth(): axial = jnp.einsum('rsq,kq->srk', total, axial_forward, precision=HIGH)  85.3 us
    reshape x6, local copies, waits for them, and re-layouts, sixth(): shaped = arrived.reshape(row_count, kt_local, rows_here, kz_local)  77.1 us
    dot_general x3, matrix products, fifth(): jnp.einsum('sa,ks->ka', arrived.reshape(NT, width), theta_forward, precis...  62.4 us
    dot_general x3, matrix products, second(): jnp.einsum('ka,sk->sa', gathered.reshape(KT, width), theta_inverse, preci...  60.9 us
    reshape x3, local copies, waits for them, and re-layouts, sixth(): jnp.transpose(shaped, (1, 3, 0, 2)).reshape(kt_local, kz_local, NR)  42.6 us

profile of v1, /device:TPU:9, one launch (start us, length us, event | category | flops | bytes accessed | tf_op | source)
XLA Modules:
  0.0 2097.2 jit_solution(10788709635123178185)
XLA Ops:
  21.4 10.8 reshape.479.refs_0_
  51.6 10.8 reshape.475.refs_0_
  62.4 71.9 %shard_map.28 = f32[8,64,3072]{2,1,0:T(8,128)} custom-call(f32[64,24576]{1,0:T(8,128)} %reshape.475.refs_0_), custom_call_target="tpu_custom_call" | custom-call | tf_op jit(solution)/shard_map/pallas_call | solution.py:116
  134.3 20.4 fusion.87.refs_1_
  174.1 10.8 reshape.474.refs_0_
  184.9 206.9 %shard_map.29 = (f32[8,64,3072]{2,1,0:T(8,128)}, f32[4,192,3072]{2,1,0:T(8,128)}) custom-call(f32[64,24576]{1,0:T(8,128)} %reshape.474.refs_0_, f32[4,192,3072]{2,1,0:T(8,128)} %fusion.87.refs_1_), custom_call_target="tpu_custom_call" | custom-call | tf_op jit(solution)/shard_map/pallas_call | solution.py:116
  391.9 20.4 fusion.86.refs_1_
  412.3 205.0 %shard_map.30 = (f32[8,64,3072]{2,1,0:T(8,128)}, f32[4,192,3072]{2,1,0:T(8,128)}) custom-call(f32[64,24576]{1,0:T(8,128)} %reshape.479.refs_0_, f32[4,192,3072]{2,1,0:T(8,128)} %fusion.86.refs_1_), custom_call_target="tpu_custom_call" | custom-call | tf_op jit(solution)/shard_map/pallas_call | solution.py:116
  617.3 20.1 fusion.85.refs_0_
  637.4 205.2 %shard_map.31 = f32[4,192,3072]{2,1,0:T(8,128)} custom-call(f32[4,192,3072]{2,1,0:T(8,128)} %fusion.85.refs_0_), custom_call_target="tpu_custom_call" | custom-call | tf_op jit(solution)/shard_map/pallas_call | solution.py:116
  842.5 11.4 copy.24
  854.0 11.3 copy.25
  865.3 28.8 %fusion.102 = f32[384,192,48]{0,1,2:T(8,128)} fusion(f32[192,48,256]{0,2,1:T(8,128)} %bitcast.259, s32[256]{0:T(256)S(1)} %and_select_fusion, pred[256]{0:T(512)(128)(4,1)S(1)} %get-tuple-element.23, pred[256]{0:T(512)(128)(4,1)S(1)} %get-tuple-element.24), kind=kOutput, calls=%fused_computation.107 | convolution fusion | flops 5436997632 | bytes 23594496 | tf_op jit(solution)/shard_map/srk,qk->rsq/dot_general | solution.py:156
  894.2 11.4 copy.21
  905.6 11.2 copy.22
  916.8 28.9 %fusion.104 = f32[384,192,48]{0,1,2:T(8,128)} fusion(f32[192,48,256]{0,2,1:T(8,128)} %bitcast.260, s32[256]{0:T(256)S(1)} %and_select_fusion, pred[256]{0:T(512)(128)(4,1)S(1)} %get-tuple-element.23, pred[256]{0:T(512)(128)(4,1)S(1)} %get-tuple-element.24), kind=kOutput, calls=%fused_computation.109 | convolution fusion | flops 5436997632 | bytes 23594496 | tf_op jit(solution)/shard_map/srk,qk->rsq/dot_general | solution.py:156
  945.8 11.4 copy.17
  957.2 11.3 copy.18
  968.5 28.6 %fusion.106 = f32[384,192,48]{0,1,2:T(8,128)} fusion(f32[192,48,256]{0,2,1:T(8,128)} %bitcast.261, s32[256]{0:T(256)S(1)} %and_select_fusion, pred[256]{0:T(512)(128)(4,1)S(1)} %get-tuple-element.23, pred[256]{0:T(512)(128)(4,1)S(1)} %get-tuple-element.24), kind=kOutput, calls=%fused_computation.111 | convolution fusion | flops 5436997632 | bytes 23594496 | tf_op jit(solution)/shard_map/srk,qk->rsq/dot_general | solution.py:156
  997.1 28.4 %fusion.54 = f32[192,48,256]{2,0,1:T(8,128)} fusion(f32[384,192,48]{0,1,2:T(8,128)} %fusion.102, f32[384,192,48]{0,1,2:T(8,128)} %fusion.104, f32[384,192,48]{0,1,2:T(8,128)} %fusion.106, bf16[9,48,192,384]{3,2,1,0:T(8,128)(2,1)} %param.3, f32[256]{0:T(256)S(1)} %select_multiply_fusion.17, s32[256]{0:T(256)S(1)} %and_select_fusion, ...), kind=kOutput, calls=%fused_computation.56 | convolution fusion | flops 5465309184 | bytes 73140736 | tf_op jit(solution)/shard_map/rsq,kq->srk/dot_general | solution.py:168
  1025.6 11.4 copy.29
  1037.0 11.3 copy.30
  1048.3 11.9 copy.31.refs_0_
  1060.3 204.3 %shard_map.32 = f32[4,192,3072]{2,1,0:T(8,128)} custom-call(f32[4,192,3072]{2,1,0:T(8,128)} %copy.31.refs_0_), custom_call_target="tpu_custom_call" | custom-call | tf_op jit(solution)/shard_map/pallas_call | solution.py:116
  1264.7 20.8 fusion.77.refs_1_
  1285.4 28.5 %fusion.57 = f32[192,48,256]{2,0,1:T(8,128)} fusion(f32[384,192,48]{0,1,2:T(8,128)} %fusion.102, f32[384,192,48]{0,1,2:T(8,128)} %fusion.104, f32[384,192,48]{0,1,2:T(8,128)} %fusion.106, bf16[9,48,192,384]{3,2,1,0:T(8,128)(2,1)} %param.3, f32[256]{0:T(256)S(1)} %select_multiply_fusion.17, s32[256]{0:T(256)S(1)} %and_select_fusion, ...), kind=kOutput, calls=%fused_computation.57 | convolution fusion | flops 5465309184 | bytes 73140736 | tf_op jit(solution)/shard_map/rsq,kq->srk/dot_general | solution.py:168
  1313.9 28.4 %fusion.51 = f32[192,48,256]{2,0,1:T(8,128)} fusion(f32[384,192,48]{0,1,2:T(8,128)} %fusion.102, f32[384,192,48]{0,1,2:T(8,128)} %fusion.104, f32[384,192,48]{0,1,2:T(8,128)} %fusion.106, bf16[9,48,192,384]{3,2,1,0:T(8,128)(2,1)} %param.3, f32[256]{0:T(256)S(1)} %select_multiply_fusion.17, s32[256]{0:T(256)S(1)} %and_select_fusion, ...), kind=kOutput, calls=%fused_computation.55 | convolution fusion | flops 5465309184 | bytes 73140736 | tf_op jit(solution)/shard_map/rsq,kq->srk/dot_general | solution.py:168
  1342.3 11.4 copy.27
  1353.7 11.3 copy.28
  1365.0 11.9 copy.32.refs_0_
  1377.0 207.0 %shard_map.33 = (f32[4,192,3072]{2,1,0:T(8,128)}, f32[8,64,3072]{2,1,0:T(8,128)}) custom-call(f32[4,192,3072]{2,1,0:T(8,128)} %copy.32.refs_0_, f32[8,64,3072]{2,1,0:T(8,128)} %fusion.77.refs_1_), custom_call_target="tpu_custom_call" | custom-call | tf_op jit(solution)/shard_map/pallas_call | solution.py:116
  1583.9 20.8 fusion.75.refs_1_
  1604.7 11.4 copy.34
  1616.1 11.3 copy.35
  1627.4 11.6 copy.36.refs_0_
  1639.0 206.3 %shard_map.34 = (f32[4,192,3072]{2,1,0:T(8,128)}, f32[8,64,3072]{2,1,0:T(8,128)}) custom-call(f32[4,192,3072]{2,1,0:T(8,128)} %copy.36.refs_0_, f32[8,64,3072]{2,1,0:T(8,128)} %fusion.75.refs_1_), custom_call_target="tpu_custom_call" | custom-call | tf_op jit(solution)/shard_map/pallas_call | solution.py:116
  1845.3 20.9 fusion.73.refs_0_
  1866.2 71.7 %shard_map.35 = f32[8,64,3072]{2,1,0:T(8,128)} custom-call(f32[8,64,3072]{2,1,0:T(8,128)} %fusion.73.refs_0_), custom_call_target="tpu_custom_call" | custom-call | tf_op jit(solution)/shard_map/pallas_call | solution.py:116
  1937.9 10.0 reshape.499
  1947.9 15.7 copy.38
  1963.6 14.0 reshape.500
  1987.3 10.0 reshape.496
  1997.2 15.7 copy.37
  2013.0 14.4 reshape.497
  2037.1 10.0 reshape.491
  2047.0 15.7 copy.33
  2062.8 14.2 reshape.492
  2086.8 10.2 pad_maximum_fusion
  (33 shorter events, 89.2 us)
Async XLA Ops:
  0.0 154.7 %copy-start.1 = (s32[384]{0:T(512)}, s32[384]{0:T(512)S(1)}, u32[]{:S(2)}) copy-start(s32[384]{0:T(512)S(1)} %multiply_add_fusion.2) | copy-start | bytes 4612
  1060.2 204.4 %copy-start.3 = (f32[8,64]{1,0:T(8,128)S(1)}, f32[8,64]{1,0:T(8,128)}, u32[]{:S(2)}) copy-start(f32[8,64]{1,0:T(8,128)} %select_multiply_fusion.16) | copy-start | bytes 6148
  1060.3 204.4 %copy-start.4 = (s32[8,64]{1,0:T(8,128)S(1)}, s32[8,64]{1,0:T(8,128)}, u32[]{:S(2)}) copy-start(s32[8,64]{1,0:T(8,128)} %add_select_fusion.6) | copy-start | bytes 6148
  1060.3 204.4 %copy-start.5 = (pred[8,64]{1,0:T(8,128)(4,1)S(1)}, pred[8,64]{1,0:T(8,128)(4,1)}, u32[]{:S(2)}) copy-start(pred[8,64]{1,0:T(8,128)(4,1)} %get-tuple-element.25) | copy-start | bytes 1540
  1060.3 204.4 %copy-start.6 = (pred[8,64]{1,0:T(8,128)(4,1)S(1)}, pred[8,64]{1,0:T(8,128)(4,1)}, u32[]{:S(2)}) copy-start(pred[8,64]{1,0:T(8,128)(4,1)} %get-tuple-element.26) | copy-start | bytes 1540
  1963.6 14.0 copy-start.2
  2076.9 9.8 copy-start
